TPU v7x, 256 devices: a whole 4x4x8 slice. The times are simulated.
256 devices in a mesh: dp: 16 (over y, x_hi, core), tensor: 16 (over z, x_lo).
Axes of the slice: x: 4 (x_hi: 2, x_lo: 2; x = x_hi * 2 + x_lo), y: 4, z: 8, core: 2. Of those that a mesh axis runs over, the one named last changes fastest.
Arguments:
- hidden: bfloat16 [8192, 8192], P('dp'), may hold values from -6 to 6
- query: bfloat16 [8192, 8192], P('dp', 'tensor'), may hold values from -300 to 300
- keys: bfloat16 [8192, 1024], P('dp', 'tensor'), may hold values from -18 to 18
- values: bfloat16 [8192, 1024], P('dp', 'tensor'), may hold values from -6 to 6
- grad_out: bfloat16 [8192, 8192], P('dp', 'tensor'), may hold values from -6 to 6
- key_weight: bfloat16 [8192, 1024], P('dp', 'tensor'), may hold values from -0.25 to 0.25
- value_weight: bfloat16 [8192, 1024], P('dp', 'tensor'), may hold values from -0.25 to 0.25
- lengths: int32 [16, 8], P('dp'), may hold values from 1 to 256, 512 in all within a row
Outputs:
- grad_query: bfloat16 [8192, 8192], P('dp', 'tensor')
- grad_hidden: bfloat16 [8192, 8192], P('dp', 'tensor')
- grad_key_weight: float32 [8192, 1024], P('dp', 'tensor')
- grad_value_weight: float32 [8192, 1024], P('dp', 'tensor')
Inputs may be any that keep to these rules, and one draw needn't show every extreme that they name: `lengths`: each row sums to 512; its largest entry is exactly 256.
All inputs are finite; a program needn't handle non-finite values.
Results may differ from a plain program's by a relative error of at most 0.017.
Values may be sent and summed in bfloat16 or wider, within the bound.
A program may use at most 128 MiB of HBM per device.

v0:
```python
import jax
import jax.numpy as jnp
from jax import lax
from jax.sharding import PartitionSpec as P


def from_partner(shard, axis, distance):
    return lax.ppermute(shard, axis, [(i, i ^ 1 << distance) for i in range(lax.axis_size(axis))])


def body(hidden, query, keys, values, grad_out, key_weight, value_weight, lengths):
    tok_count = hidden.shape[0]
    half_size = keys.shape[1]
    head_size = 2 * half_size
    local_heads = query.shape[1] // head_size
    lower_half = lax.axis_index("tensor") % 2 == 0
    other_keys, other_values = from_partner((keys, values), "tensor", 0)
    key_head = jnp.where(
        lower_half, jnp.concatenate([keys, other_keys], 1), jnp.concatenate([other_keys, keys], 1)
    )
    value_head = jnp.where(
        lower_half,
        jnp.concatenate([values, other_values], 1),
        jnp.concatenate([other_values, values], 1),
    )
    query_three = query.reshape(tok_count, local_heads, head_size)
    grad_three = grad_out.reshape(tok_count, local_heads, head_size)
    positions = jnp.arange(tok_count, dtype=jnp.int32)
    bounds = jnp.cumsum(lengths[0])
    segment = jnp.sum((positions[:, None] >= bounds[None, :]).astype(jnp.int32), axis=1)
    allowed = (segment[:, None] == segment[None, :]) & (positions[None, :] <= positions[:, None])
    score_scale = head_size ** (-0.5)
    scores = (
        jnp.einsum("ihd,jd->hij", query_three, key_head, preferred_element_type=jnp.float32)
        * score_scale
    )
    scores = jnp.where(allowed[None], scores, -jnp.inf)
    top_score = jnp.max(scores, axis=-1, keepdims=True)
    expo = jnp.exp(scores - top_score)
    attn_probs = expo / jnp.sum(expo, axis=-1, keepdims=True)
    probs_low = attn_probs.astype(jnp.bfloat16)
    attended = jnp.einsum("hij,jd->ihd", probs_low, value_head, preferred_element_type=jnp.float32)
    row_delta = jnp.sum(grad_three.astype(jnp.float32) * attended, axis=-1)
    dprobs = jnp.einsum("ihd,jd->hij", grad_three, value_head, preferred_element_type=jnp.float32)
    dscores = (attn_probs * (dprobs - jnp.transpose(row_delta)[:, :, None]) * score_scale).astype(
        jnp.bfloat16
    )
    grad_query = jnp.einsum("hij,jd->ihd", dscores, key_head, preferred_element_type=jnp.float32)
    grad_query = grad_query.astype(jnp.bfloat16).reshape(tok_count, local_heads * head_size)
    key_part = jnp.einsum("hij,ihd->jd", dscores, query_three, preferred_element_type=jnp.float32)
    value_part = jnp.einsum(
        "hij,ihd->jd", probs_low, grad_three, preferred_element_type=jnp.float32
    )
    keep_key = jnp.where(lower_half, key_part[:, :half_size], key_part[:, half_size:])
    send_key = jnp.where(lower_half, key_part[:, half_size:], key_part[:, :half_size])
    keep_value = jnp.where(lower_half, value_part[:, :half_size], value_part[:, half_size:])
    send_value = jnp.where(lower_half, value_part[:, half_size:], value_part[:, :half_size])
    got_key, got_value = from_partner((send_key, send_value), "tensor", 0)
    key_grad = (keep_key + got_key).astype(jnp.bfloat16)
    value_grad = (keep_value + got_value).astype(jnp.bfloat16)
    both_grads = jnp.concatenate([key_grad, value_grad], 1)
    weight_share = lax.psum_scatter(
        jnp.einsum("td,tc->dc", hidden, both_grads, preferred_element_type=jnp.float32).astype(
            jnp.bfloat16
        ),
        "dp",
        scatter_dimension=0,
        tiled=True,
    ).astype(jnp.float32)
    grad_key_weight = weight_share[:, :half_size]
    grad_value_weight = weight_share[:, half_size:]
    full_key_w, full_value_w = (
        lax.all_gather(key_weight, "dp", axis=0, tiled=True),
        lax.all_gather(value_weight, "dp", axis=0, tiled=True),
    )
    both_weights = jnp.concatenate([full_key_w, full_value_w], 1)
    partial_term = jnp.einsum(
        "tc,dc->td", both_grads, both_weights, preferred_element_type=jnp.float32
    )
    grad_hidden = lax.psum_scatter(partial_term, "tensor", scatter_dimension=1, tiled=True).astype(
        jnp.bfloat16
    )
    return (grad_query, grad_hidden, grad_key_weight, grad_value_weight)


def solution(mesh):
    placed = (
        P("dp", None),
        P("dp", "tensor"),
        P("dp", "tensor"),
        P("dp", "tensor"),
        P("dp", "tensor"),
        P("dp", "tensor"),
        P("dp", "tensor"),
        P("dp", None),
    )
    return jax.shard_map(
        body,
        mesh=mesh,
        in_specs=placed,
        out_specs=(P("dp", "tensor"), P("dp", "tensor"), P("dp", "tensor"), P("dp", "tensor")),
        check_vma=False,
    )
```

profile of v0, /device:TPU:32, one launch (start us, length us, event | category | flops | bytes accessed | tf_op | source)
XLA Modules:
  0.0 556.3 jit_solution(11031641530412204621)
XLA Ops:
  7.2 0.0 all-gather.5.cloned.1.call-start
  7.2 0.7 all-gather.5.cloned.1.call-update
  7.9 0.0 all-gather.3.cloned.1.call-start
  7.9 1.6 collective-permute-start
  9.5 0.5 collective-permute-start.1
  10.1 0.0 all-gather.3.cloned.1.call-update
  10.1 0.0 reduce-scatter.5.cloned.1.call-start
  10.1 0.8 reduce-window.8
  11.0 0.1 convert_reduce_fusion
  11.1 0.2 fusion.16
  11.3 1.3 copy.25
  12.5 1.3 copy.43
  13.8 0.0 collective-permute-done
  13.8 4.5 fusion.43
  18.3 0.0 copy-start.2
  18.3 2.8 fusion.13
  21.2 0.0 copy-start
  21.2 0.8 convolution_bitcast_fusion.1
  22.0 1.6 collective-permute-start.3
  23.6 0.0 collective-permute-done.1
  23.6 0.0 copy-done.2
  23.6 0.0 slice-start
  23.6 0.5 fusion.15
  24.1 0.0 copy-done
  24.1 0.0 slice-start.1
  24.1 0.9 fusion.4
  25.0 0.8 convolution_bitcast_fusion.2
  25.8 0.8 collective-permute-start.2
  26.6 0.4 collective-permute-done.3
  27.1 3.9 collective-permute-done.2
  31.0 0.0 slice-done
  31.0 0.0 slice-done.1
  31.0 2.6 fusion.1
  33.6 0.0 reduce-scatter.5.cloned.1.call-update
  33.6 0.0 reduce-scatter.3.cloned.1.call-start
  33.7 27.5 %all-gather.5.cloned.1.call-done = bf16[8192,64]{0,1:T(8,128)(2,1)} async-done(((bf16[512,64]{0,1:T(8,128)(2,1)}), bf16[8192,64]{0,1:T(8,128)(2,1)}) %all-gather.5.cloned.1.call-update) | async-done | bytes 1048592 | tf_op jit(solution)/shard_map/all_gather | solution.py:74
  61.2 50.5 %all-gather.3.cloned.1.call-done = bf16[8192,64]{0,1:T(8,128)(2,1)} async-done(((bf16[512,64]{0,1:T(8,128)(2,1)}), bf16[8192,64]{0,1:T(8,128)(2,1)}) %all-gather.3.cloned.1.call-update) | async-done | bytes 1048592 | tf_op jit(solution)/shard_map/all_gather | solution.py:73
  111.7 9.6 %fusion.6 = f32[512,8192]{1,0:T(8,128)} fusion(bf16[8192,64]{0,1:T(8,128)(2,1)} %all-gather.5.cloned.1.call-done, bf16[8192,64]{0,1:T(8,128)(2,1)} %all-gather.3.cloned.1.call-done, bf16[512,64]{0,1:T(8,128)(2,1)S(1)} %add_convert_fusion, bf16[512,64]{0,1:T(8,128)(2,1)S(1)} %add_convert_fusion.1), kind=kOutput, calls=%fused_computation.10 | convolution fusion | flops 1078198272 | bytes 19005440 | tf_op jit(solution)/shard_map/tc,dc->td/dot_general | solution.py:77
  121.3 0.0 copy-start.1
  121.3 0.0 reduce-scatter.3.cloned.1.call-update
  121.4 0.8 copy-done.1
  122.2 0.4 convolution_convert_fusion.1
  122.6 1.0 copy.33
  123.6 70.9 %reduce-scatter.5.cloned.1.call-done = bf16[512,128]{0,1:T(8,128)(2,1)} async-done(((bf16[8192,128]{0,1:T(8,128)(2,1)}), bf16[512,128]{0,1:T(8,128)(2,1)}) %reduce-scatter.5.cloned.1.call-update) | async-done | bytes 131088 | tf_op jit(solution)/shard_map/reduce_scatter | solution.py:62
  194.6 1.6 fusion.42
  196.2 351.5 %reduce-scatter.3.cloned.1.call-done = f32[512,512]{1,0:T(8,128)} async-done(((f32[512,8192]{1,0:T(8,128)}), f32[512,512]{1,0:T(8,128)}) %reduce-scatter.3.cloned.1.call-update) | async-done | bytes 1048592 | tf_op jit(solution)/shard_map/reduce_scatter | solution.py:80
  547.7 2.1 convert_element_type.44
  (5 shorter events, 0.1 us)
Async XLA Ops:
  7.2 54.0 %all-gather.5.cloned.1.call-start = ((), (), s32[]{:S(2)}) async-start(), calls=%async_computation.3 | async-start | bytes 1114112 | tf_op jit(solution)/shard_map/all_gather | solution.py:74
  7.9 103.8 %all-gather.3.cloned.1.call-start = ((), (), s32[]{:S(2)}) async-start(), calls=%async_computation.2 | async-start | bytes 1114112 | tf_op jit(solution)/shard_map/all_gather | solution.py:73
  7.9 5.9 %collective-permute-start = (bf16[512,64]{0,1:T(8,128)(2,1)}, bf16[512,64]{0,1:T(8,128)(2,1)S(1)}, u32[]{:S(2)}, u32[]{:S(2)}) collective-permute-start(bf16[512,64]{0,1:T(8,128)(2,1)} %param.10), channel_id=1, source_target_pairs={{0,1},{1,0},{2,3},{3,2},{4,5},{5,4},{6,7},{7,6},{8,9},{9,8},{10,11... | collective-permute-start | bytes 196616 | tf_op jit(solution)/shard_map/ppermute | solution.py:8
  9.5 14.1 %collective-permute-start.1 = (bf16[512,64]{0,1:T(8,128)(2,1)}, bf16[512,64]{0,1:T(8,128)(2,1)S(1)}, u32[]{:S(2)}, u32[]{:S(2)}) collective-permute-start(bf16[512,64]{0,1:T(8,128)(2,1)} %param.11), channel_id=1, source_target_pairs={{0,1},{1,0},{2,3},{3,2},{4,5},{5,4},{6,7},{7,6},{8,9},{9,8},{10,11... | collective-permute-start | bytes 196616 | tf_op jit(solution)/shard_map/ppermute | solution.py:8
  10.1 184.5 %reduce-scatter.5.cloned.1.call-start = ((), (), s32[]{:S(2)}) async-start(), calls=%async_computation.5 | async-start | bytes 2228224 | tf_op jit(solution)/shard_map/reduce_scatter | solution.py:62
  18.3 5.2 copy-start.2
  21.2 2.9 copy-start
  22.0 5.1 collective-permute-start.3
  23.6 7.4 %slice-start = ((s8[8388608]{0:T(1024)(128)(4,1)}), s8[4194304]{0:T(1024)(128)(4,1)S(1)}, s32[]{:S(2)}) async-start(s8[8388608]{0:T(1024)(128)(4,1)} %bitcast.68), calls=%async_computation.6 | async-start | bytes 8388608
  24.1 6.9 %slice-start.1 = ((s8[8388608]{0:T(1024)(128)(4,1)}), s8[4194304]{0:T(1024)(128)(4,1)S(1)}, s32[]{:S(2)}) async-start(s8[8388608]{0:T(1024)(128)(4,1)} %bitcast.68), calls=%async_computation.7 | async-start | bytes 8388608
  25.8 5.2 collective-permute-start.2
  33.6 514.1 %reduce-scatter.3.cloned.1.call-start = ((), (), s32[]{:S(2)}) async-start(), calls=%async_computation.4 | async-start | bytes 17825792 | tf_op jit(solution)/shard_map/reduce_scatter | solution.py:80
  121.3 0.8 copy-start.1
Sparse Core Ops, SparseCore 0:
  10.6 50.5 all-gather.4
  63.8 47.8 all-gather.2
  115.9 78.6 reduce-scatter.4
  197.2 350.4 reduce-scatter.2
where the time goes:
time: 558 us; the launch traced here: 556 us
  waiting for transfers between devices  506 us (91%)
  matrix products  20.1 us (4%)
  between operations  13.9 us (2%)
  other arithmetic  6.11 us (1%)
  local copies, waits for them, and re-layouts  5.94 us (1%)
    reduce_scatter x1, waiting for transfers between devices, body(): lax.psum_scatter(partial_term, 'tensor', scatter_dimension=1, tiled=True)  352 us
    reduce_scatter x1, waiting for transfers between devices, body(): lax.psum_scatter(jnp.einsum('td,tc->dc', hidden, both_grads, preferred_el...  70.9 us
    all_gather x1, waiting for transfers between devices, body(): lax.all_gather(key_weight, 'dp', axis=0, tiled=True)  50.5 us
    all_gather x1, waiting for transfers between devices, body(): lax.all_gather(value_weight, 'dp', axis=0, tiled=True)  27.5 us
  transfers between devices with their start and end apart: 8, of which 6 were waited for; matrix products, arithmetic and copies ran while one was open for 5% of the time, Pallas kernels for 0%

commit v1 on v0

v1 whole, which is shorter than its diff:
```python
import functools

import jax
import jax.numpy as jnp
from jax import lax
from jax.experimental import pallas as pl
from jax.experimental.pallas import tpu as pltpu
from jax.sharding import PartitionSpec as P

MESH = pl.DeviceIdType.MESH
F32 = jnp.float32
BF16 = jnp.bfloat16
TOK = 512
HEAD = 128
HALF = 64
HEADS = 4
ROWS = 128
STEPS = TOK // ROWS
FEAT = 512
NEG = -1e30

NT = (((1,), (1,)), ((), ()))
NN = (((1,), (0,)), ((), ()))
TN = (((0,), (0,)), ((), ()))


def dot(a, b, dims):
    return lax.dot_general(a, b, dims, preferred_element_type=F32)


NUMBER = {}
for name, count in (
    ("kv", 1),
    ("w_turn", 1),
    ("w_xh", 1),
    ("w_y", 6),
    ("w_core", 8),
    ("hid", 8),
    ("part", STEPS),
    ("kg_core", 2),
    ("ring_right", 8),
    ("ring_left", 8),
    ("c_y", 6),
    ("c_xh", 1),
    ("b_xl", STEPS),
):
    NUMBER[name] = sum(n for _, n in NUMBER.values()), count
N_REMOTE = sum(n for _, n in NUMBER.values())
LOCAL = {"k": 0, "v": 1, "kw": 2, "vw": 3, "q": 4, "go": 5, "hid": 6, "gq": 14, "gh": 15, "gk": 19, "gv": 20}
N_LOCAL = 21


def kernel(
    len_ref, hid_hbm, q_hbm, k_hbm, v_hbm, go_hbm, kw_hbm, vw_hbm,
    gq_hbm, gh_hbm, gk_hbm, gv_hbm,
    k_half, v_half, kw_half, vw_half, kv, key_buf, val_buf, q_buf, go_buf, gq_buf,
    w_own, w_all, hid_buf, dk_acc, dv_acc, part_send, part_got, keep_buf,
    kg_all, kg_other, kg_turned, c_send, c_got, c_own, cx_send, cx_got,
    b_send, b_got, b_own, gh_buf, gk_buf, gv_buf,
    send_sem, recv_sem, local_sem,
):
    dp, tensor = lax.axis_index("dp"), lax.axis_index("tensor")
    core, chip = lax.rem(dp, 2), dp // 2
    xh, y = lax.rem(chip, 2), chip // 2
    xl, z = lax.rem(tensor, 2), tensor // 2

    def at(y=y, xh=xh, core=core, z=z, xl=xl):
        return ((y * 2 + xh) * 2 + core, z * 2 + xl)

    def y_plus(k):
        return lax.rem(y + k, 4)

    def z_plus(k):
        return lax.rem(z + k + 8, 8)

    to_xl, to_core, to_xh = at(xl=1 - xl), at(core=1 - core), at(xh=1 - xh)
    to_right, to_left = at(z=z_plus(1)), at(z=z_plus(-1))
    to_y = [at(y=y_plus(k)) for k in (1, 2, 3)]
    to_turned = at(y=z // 2, xh=lax.rem(z, 2), z=chip)
    turned_away = chip != z

    def local(src, dst, number):
        copy = pltpu.make_async_copy(src, dst, local_sem.at[number])
        copy.start()
        return copy

    started = []

    def remote(src, dst, name, number, device):
        first, count = NUMBER[name]
        assert 0 <= number < count
        copy = pltpu.make_async_remote_copy(
            src_ref=src, dst_ref=dst, send_sem=send_sem.at[first + number],
            recv_sem=recv_sem.at[first + number], device_id=device, device_id_type=MESH,
        )
        return copy

    def send(*args):
        copy = remote(*args)
        copy.start()
        started.append(copy)

    def arrived(dst, name, number):
        first, _ = NUMBER[name]
        pltpu.make_async_remote_copy(
            src_ref=dst, dst_ref=dst, send_sem=send_sem.at[first + number],
            recv_sem=recv_sem.at[first + number], device_id=to_core, device_id_type=MESH,
        ).wait_recv()

    in_k = local(k_hbm, k_half, LOCAL["k"])
    in_v = local(v_hbm, v_half, LOCAL["v"])
    barrier = pltpu.get_barrier_semaphore()
    for device in [to_xl, to_core, to_xh, to_right, to_left] + to_y:
        pl.semaphore_signal(barrier, inc=1, device_id=device, device_id_type=MESH)

    @pl.when(turned_away)
    def _():
        pl.semaphore_signal(barrier, inc=1, device_id=to_turned, device_id_type=MESH)

    in_kw = local(kw_hbm, kw_half, LOCAL["kw"])
    in_vw = local(vw_hbm, vw_half, LOCAL["vw"])
    in_q = local(q_hbm, q_buf, LOCAL["q"])
    in_go = local(go_hbm, go_buf, LOCAL["go"])
    in_hid = []
    for block in range(8):
        columns = pl.ds(pl.multiple_of((2 * block + core) * FEAT, FEAT), FEAT)
        in_hid.append(local(hid_hbm.at[:, columns], hid_buf.at[block, 0], LOCAL["hid"] + block))
    in_k.wait()
    in_v.wait()
    kv[0] = jnp.concatenate([k_half[...], v_half[...]], axis=1)
    in_kw.wait()
    in_vw.wait()
    w_own[...] = jnp.concatenate([kw_half[...], vw_half[...]], axis=1)
    pl.semaphore_wait(barrier, 8 + jnp.where(turned_away, 1, 0))

    send(kv.at[0], kv.at[1], "kv", 0, to_xl)

    turn = remote(w_own, w_all.at[z, core], "w_turn", 0, to_turned)

    @pl.when(turned_away)
    def _():
        turn.start()

    for block in range(8):
        columns = pl.ds(pl.multiple_of((2 * block + 1 - core) * FEAT, FEAT), FEAT)
        send(hid_hbm.at[:, columns], hid_buf.at[block, 1], "hid", block, to_core)

    lane = lax.broadcasted_iota(jnp.int32, (1, HEADS * ROWS), 1) % ROWS
    bounds, total = [], 0
    for k in range(8):
        total = total + len_ref[0, k]
        bounds.append(total)

    def first_key(rows):
        start = jnp.zeros_like(rows)
        for bound in bounds:
            start = jnp.where(rows >= bound, bound, start)
        return start

    half_lane = lax.broadcasted_iota(jnp.int32, (1, HEAD), 1) < HALF
    lower = xl == 0
    dk_acc[...] = jnp.zeros_like(dk_acc)
    dv_acc[...] = jnp.zeros_like(dv_acc)

    arrived(kv.at[1], "kv", 0)
    own, other = kv[0].astype(F32), kv[1].astype(F32)
    first, second = jnp.where(lower, own, other), jnp.where(lower, other, own)
    key_buf[...] = jnp.where(half_lane, first, pltpu.roll(second, HALF, 1)).astype(BF16)
    val_buf[...] = jnp.where(half_lane, pltpu.roll(first, HALF, 1), second).astype(BF16)
    in_q.wait()
    in_go.wait()

    scale = HEAD ** -0.5
    to_exp2 = scale * 1.4426950408889634

    def heads_of(ref, step):
        return jnp.concatenate(
            [ref[pl.ds(step * ROWS, ROWS), pl.ds(h * HEAD, HEAD)] for h in range(HEADS)], axis=0
        )

    def attention(step):
        low, high = max(0, step - 2) * ROWS, (step + 1) * ROWS
        width = high - low
        seen = pl.ds(low, width)
        rows = lane + step * ROWS
        keys, vals = key_buf[seen, :], val_buf[seen, :]
        queries, grads = heads_of(q_buf, step), heads_of(go_buf, step)
        key_at = low + lax.broadcasted_iota(jnp.int32, (width, HEADS * ROWS), 0)
        allowed = (key_at >= first_key(rows)) & (key_at <= rows)
        scores = jnp.where(allowed, dot(keys, queries, NT), NEG)
        top = jnp.max(scores, axis=0, keepdims=True)
        expo = jnp.exp2((scores - top) * to_exp2)
        probs = expo * (1.0 / jnp.sum(expo, axis=0, keepdims=True))
        probs_low = probs.astype(BF16)
        dprobs = dot(vals, grads, NT)
        delta = jnp.sum(probs_low.astype(F32) * dprobs, axis=0, keepdims=True)
        dscores = (probs * (dprobs - delta) * scale).astype(BF16)
        grad_q = dot(dscores, keys, TN).astype(BF16)
        for h in range(HEADS):
            gq_buf[pl.ds(step * ROWS, ROWS), pl.ds(h * HEAD, HEAD)] = grad_q[h * ROWS:(h + 1) * ROWS]
        dk_acc[seen, :] += dot(dscores, queries, NN)
        dv_acc[seen, :] += dot(probs_low, grads, NN)
        done = pl.ds(step * ROWS, ROWS)
        dk, dv = dk_acc[done, :], dv_acc[done, :]
        lower_part = jnp.where(half_lane, dk, pltpu.roll(dv, HALF, 1))
        upper_part = jnp.where(half_lane, pltpu.roll(dk, HALF, 1), dv)
        keep_buf[done, :] = jnp.where(lower, lower_part, upper_part)
        part_send[done, :] = jnp.where(lower, upper_part, lower_part).astype(BF16)
        send(part_send.at[done], part_got.at[done], "part", step, to_xl)

    def finish(step):
        done = pl.ds(step * ROWS, ROWS)
        arrived(part_got.at[done], "part", step)
        kg_all[z, done, :] = (keep_buf[done, :] + part_got[done, :].astype(F32)).astype(BF16)

    def half_rows(half):
        return pl.ds(half * (TOK // 2), TOK // 2)

    def ring_hops(half):
        return (4, 3) if half == 1 else (3, 4)

    def ring_send(half, hop):
        rows = half_rows(half)
        right, left = ring_hops(half)
        if hop < right:
            block = kg_all.at[z_plus(-hop), rows]
            send(block, block, "ring_right", half * 4 + hop, to_right)
        if hop < left:
            block = kg_all.at[z_plus(hop), rows]
            send(block, block, "ring_left", half * 4 + hop, to_left)

    def ring_wait(half, hop):
        rows = half_rows(half)
        right, left = ring_hops(half)
        if hop < right:
            arrived(kg_all.at[z_plus(-hop - 1), rows], "ring_right", half * 4 + hop)
        if hop < left:
            arrived(kg_all.at[z_plus(hop + 1), rows], "ring_left", half * 4 + hop)

    def kg_start(half):
        rows = half_rows(half)
        ring_send(half, 0)
        send(kg_all.at[z, rows], kg_other.at[rows], "kg_core", half, to_core)

    def w_to_y(block, number):
        ref = w_all.at[block, core]
        for k in range(3):
            send(ref, ref, "w_y", number * 3 + k, to_y[k])

    def w_to_core(block, number):
        ref = w_all.at[block, core]
        send(ref, ref, "w_core", number, to_core)

    attention(3)

    @pl.when(turned_away)
    def _():
        arrived(w_all.at[chip, core], "w_turn", 0)

    @pl.when(jnp.logical_not(turned_away))
    def _():
        w_all[chip, core] = w_own[...]

    ref = w_all.at[chip, core]
    send(ref, ref, "w_xh", 0, to_xh)
    w_to_y(chip, 0)
    w_to_core(chip, 0)

    attention(2)
    attention(1)
    finish(3)
    finish(2)
    kg_start(1)
    chip_xh = y * 2 + 1 - xh
    arrived(w_all.at[chip_xh, core], "w_xh", 0)
    w_to_y(chip_xh, 1)
    w_to_core(chip_xh, 1)
    attention(0)
    out_gq = local(gq_buf, gq_hbm, LOCAL["gq"])
    finish(1)
    finish(0)
    kg_start(0)
    ring_wait(1, 0)
    ring_send(1, 1)

    for block in range(8):
        in_hid[block].wait()
        arrived(hid_buf.at[block, 1], "hid", block)
    arrived(kg_other.at[half_rows(1)], "kg_core", 1)
    arrived(kg_other.at[half_rows(0)], "kg_core", 0)
    kg_turned[:, pl.ds(0, TOK)] = kg_all[z].T
    kg_turned[:, pl.ds(TOK, TOK)] = kg_other[...].T

    def weight_grad(block):
        hid = hid_buf[block].reshape(2 * TOK, FEAT)
        return dot(kg_turned[...], hid, NN)

    def c_round(kind, x_high):
        for k in (2, 1, 3):
            number = kind * 3 + k - 1
            c_send[number] = weight_grad(y_plus(k) * 2 + x_high).astype(BF16)
            send(c_send.at[number], c_got.at[number], "c_y", number, to_y[k - 1])

    def c_sum(kind):
        total = c_own[kind]
        for k in range(3):
            arrived(c_got.at[kind * 3 + k], "c_y", kind * 3 + k)
            total = total + c_got[kind * 3 + k].astype(F32)
        return total

    c_round(0, 1 - xh)
    c_round(1, xh)
    ring_wait(0, 0)
    ring_send(0, 1)
    ring_wait(1, 1)
    ring_send(1, 2)
    c_own[0] = weight_grad(y * 2 + 1 - xh)
    c_own[1] = weight_grad(y * 2 + xh)
    ring_wait(0, 1)
    ring_send(0, 2)
    for k in range(3):
        for number, x_high in ((0, xh), (1, 1 - xh)):
            block = lax.rem(y - k - 1 + 4, 4) * 2 + x_high
            arrived(w_all.at[block, core], "w_y", number * 3 + k)
            w_to_core(block, 2 + number * 3 + k)
    ring_wait(1, 2)
    ring_send(1, 3)
    cx_send[...] = c_sum(0).astype(BF16)
    send(cx_send, cx_got, "c_xh", 0, to_xh)
    ring_wait(0, 2)
    ring_send(0, 3)
    arrived(w_all.at[chip, 1 - core], "w_core", 0)
    arrived(w_all.at[chip_xh, 1 - core], "w_core", 1)
    for k in range(3):
        for number, x_high in ((0, xh), (1, 1 - xh)):
            block = lax.rem(y - k - 1 + 4, 4) * 2 + x_high
            arrived(w_all.at[block, 1 - core], "w_core", 2 + number * 3 + k)

    def all_heads(rows):
        return jnp.concatenate([kg_all[head, rows, :] for head in range(8)], axis=1)

    def features(kind):
        return jnp.concatenate([w_all[head, kind] for head in range(8)], axis=1)

    def hidden_grad(half):
        for step in (2 * half + 1, 2 * half):
            rows = pl.ds(step * ROWS, ROWS)
            b_send[rows, :] = dot(all_heads(rows), features(1 - xl), NT).astype(BF16)
            send(b_send.at[rows], b_got.at[rows], "b_xl", step, to_xl)
        rows = half_rows(half)
        b_own[rows, :] = dot(all_heads(rows), features(xl), NT)

    ring_wait(1, 3)
    hidden_grad(1)
    ring_wait(0, 3)
    hidden_grad(0)

    mine = c_sum(1)
    arrived(cx_got, "c_xh", 0)
    mine = mine + cx_got[...].astype(F32)
    gk_buf[...] = mine[:HALF].T
    gv_buf[...] = mine[HALF:].T
    outs = [out_gq, local(gk_buf, gk_hbm, LOCAL["gk"]), local(gv_buf, gv_hbm, LOCAL["gv"])]
    for step in (3, 2, 1, 0):
        rows = pl.ds(step * ROWS, ROWS)
        arrived(b_got.at[rows], "b_xl", step)
        gh_buf[rows, :] = (b_own[rows, :] + b_got[rows, :].astype(F32)).astype(BF16)
        outs.append(local(gh_buf.at[rows], gh_hbm.at[rows], LOCAL["gh"] + step))
    for copy in outs:
        copy.wait()
    for copy in started:
        copy.wait_send()

    @pl.when(turned_away)
    def _():
        turn.wait_send()


def body(hidden, query, keys, values, grad_out, key_weight, value_weight, lengths):
    anywhere = pl.BlockSpec(memory_space=pl.ANY)

    def vmem(*shape, dtype=BF16):
        return pltpu.VMEM(shape, dtype)

    return pl.pallas_call(
        kernel,
        out_shape=(
            jax.ShapeDtypeStruct((TOK, HEADS * HEAD), BF16),
            jax.ShapeDtypeStruct((TOK, FEAT), BF16),
            jax.ShapeDtypeStruct((FEAT, HALF), F32),
            jax.ShapeDtypeStruct((FEAT, HALF), F32),
        ),
        in_specs=[pl.BlockSpec(memory_space=pltpu.SMEM)] + [anywhere] * 7,
        out_specs=(anywhere,) * 4,
        scratch_shapes=[
            vmem(TOK, HALF), vmem(TOK, HALF), vmem(FEAT, HALF), vmem(FEAT, HALF),
            vmem(2, TOK, HEAD), vmem(TOK, HEAD), vmem(TOK, HEAD),
            vmem(TOK, HEADS * HEAD), vmem(TOK, HEADS * HEAD), vmem(TOK, HEADS * HEAD),
            vmem(FEAT, HEAD), vmem(8, 2, FEAT, HEAD), vmem(8, 2, TOK, FEAT),
            vmem(TOK, HEAD, dtype=F32), vmem(TOK, HEAD, dtype=F32),
            vmem(TOK, HEAD), vmem(TOK, HEAD), vmem(TOK, HEAD, dtype=F32),
            vmem(8, TOK, HEAD), vmem(TOK, HEAD), vmem(HEAD, 2 * TOK),
            vmem(6, HEAD, FEAT), vmem(6, HEAD, FEAT), vmem(2, HEAD, FEAT, dtype=F32),
            vmem(HEAD, FEAT), vmem(HEAD, FEAT),
            vmem(TOK, FEAT), vmem(TOK, FEAT), vmem(TOK, FEAT, dtype=F32), vmem(TOK, FEAT),
            vmem(FEAT, HALF, dtype=F32), vmem(FEAT, HALF, dtype=F32),
            pltpu.SemaphoreType.DMA((N_REMOTE,)), pltpu.SemaphoreType.DMA((N_REMOTE,)),
            pltpu.SemaphoreType.DMA((N_LOCAL,)),
        ],
        compiler_params=pltpu.CompilerParams(
            collective_id=0, has_side_effects=True, vmem_limit_bytes=48 * 1024 * 1024
        ),
        name="attention_backward",
    )(lengths, hidden, query, keys, values, grad_out, key_weight, value_weight)


def solution(mesh):
    placed = (
        P("dp", None),
        P("dp", "tensor"),
        P("dp", "tensor"),
        P("dp", "tensor"),
        P("dp", "tensor"),
        P("dp", "tensor"),
        P("dp", "tensor"),
        P("dp", None),
    )
    return jax.shard_map(
        body,
        mesh=mesh,
        in_specs=placed,
        out_specs=(P("dp", "tensor"), P("dp", "tensor"), P("dp", "tensor"), P("dp", "tensor")),
        check_vma=False,
    )
```

time: 558 us -> 74.3 us (0.13)
  waiting for transfers between devices: 506 us -> 0 us
  Pallas kernels: 0 us -> 63.5 us
  matrix products: 20.1 us -> 0 us
  between operations: 13.9 us -> 0.68 us
  other arithmetic: 6.11 us -> 0 us
    reduce_scatter x2 -> x0, waiting for transfers between devices: 422 us -> none  [the longest x1 352 us: body(): lax.psum_scatter(partial_term, 'tensor', scatter_dimension=1, tiled=True)]
    all_gather x2 -> x0, waiting for transfers between devices: 78 us -> none  [the longest x1 50.5 us: body(): lax.all_gather(key_weight, 'dp', axis=0, tiled=True)]
    pallas_call x0 -> x1, Pallas kernels: none -> 63.5 us  [body(): pl.pallas_call(kernel, out_shape=(jax.ShapeDtypeStruct((TOK, HEADS * HEAD...]
    dot_general x7 -> x0, matrix products: 15.6 us -> none  [the longest x1 9.63 us: body(): jnp.einsum('tc,dc->td', both_grads, both_weights, preferred_element_type=...]
  transfers between devices with their start and end apart: 8 -> 0, of which waited for: 6 -> 0; matrix products, arithmetic and copies ran while one was open for 5% -> 0% of each run, Pallas kernels for 0% -> 0%
where the time goes in v1:
time: 74.3 us; the launch traced here: 73.9 us
  Pallas kernels  63.5 us (85%)
  local copies, waits for them, and re-layouts  9.7 us (13%)
    pallas_call x1, Pallas kernels, body(): pl.pallas_call(kernel, out_shape=(jax.ShapeDtypeStruct((TOK, HEADS * HEAD...  63.5 us
    unnamed x12, local copies, waits for them, and re-layouts  8.16 us
    pallas_call x2, local copies, waits for them, and re-layouts, body(): pl.pallas_call(kernel, out_shape=(jax.ShapeDtypeStruct((TOK, HEADS * HEAD...  1.54 us

profile of v1, /device:TPU:32, one launch (start us, length us, event | category | flops | bytes accessed | tf_op | source)
XLA Modules:
  0.0 73.9 jit_solution(9578858187312761396)
XLA Ops:
  0.6 1.0 %copy.12.k_hbm = bf16[512,64]{1,0:T(8,128)(2,1)S(1)} copy(bf16[512,64]{0,1:T(8,128)(2,1)} %param.10) | data formatting | bytes 131072 | tf_op args[2]
  1.6 1.0 %copy.13.v_hbm = bf16[512,64]{1,0:T(8,128)(2,1)S(1)} copy(bf16[512,64]{0,1:T(8,128)(2,1)} %param.11) | data formatting | bytes 131072 | tf_op args[3]
  2.6 1.0 %copy.14.kw_hbm = bf16[512,64]{1,0:T(8,128)(2,1)S(1)} copy(bf16[512,64]{0,1:T(8,128)(2,1)} %param.13) | data formatting | bytes 131072 | tf_op args[5]
  3.5 1.0 %copy.15.vw_hbm = bf16[512,64]{1,0:T(8,128)(2,1)S(1)} copy(bf16[512,64]{0,1:T(8,128)(2,1)} %param.14) | data formatting | bytes 131072 | tf_op args[6]
  4.5 0.0 copy-start
  4.5 1.0 %copy-done = bf16[512,512]{1,0:T(8,128)(2,1)S(1)} copy-done((bf16[512,512]{1,0:T(8,128)(2,1)S(1)}, bf16[512,512]{1,0:T(8,128)(2,1)}, u32[]{:S(2)}) %copy-start) | copy-done | bytes 524312
  5.5 0.0 copy-start.1
  5.5 1.0 %copy-done.1 = bf16[512,512]{1,0:T(8,128)(2,1)S(1)} copy-done((bf16[512,512]{1,0:T(8,128)(2,1)S(1)}, bf16[512,512]{1,0:T(8,128)(2,1)}, u32[]{:S(2)}) %copy-start.1) | copy-done | bytes 524312
  6.6 0.0 copy-start.2
  6.6 0.7 copy-done.2
  7.2 63.5 %attention_backward.1 = (bf16[512,512]{1,0:T(8,128)(2,1)S(1)}, bf16[512,512]{1,0:T(8,128)(2,1)S(1)}, f32[512,64]{1,0:T(8,128)S(1)}, f32[512,64]{1,0:T(8,128)S(1)}) custom-call(s32[1,8]{1,0:T(1,128)S(1)} %copy-done.2, bf16[512,8192]{1,0:T(8,128)(2,1)} %hid_hbm.1, bf16[512,512]{1,0:T(8,128)(2,1)S(1)} %copy-done, bf16[512,64]{1,0:T(8,128)(2,1)S(1)} %copy.12.k_hbm, ...), custom_call_target="tpu_custom_call" | custom-call | tf_op jit(solution)/shard_map/attention_backward/pallas_call | solution.py:385
  70.8 0.8 %copy.16 = f32[512,64]{0,1:T(8,128)} copy(f32[512,64]{1,0:T(8,128)S(1)} %get-tuple-element.6) | data formatting | bytes 262144 | tf_op jit(solution)/shard_map/attention_backward/pallas_call | solution.py:385
  71.6 0.8 %copy.17 = f32[512,64]{0,1:T(8,128)} copy(f32[512,64]{1,0:T(8,128)S(1)} %get-tuple-element.7) | data formatting | bytes 262144 | tf_op jit(solution)/shard_map/attention_backward/pallas_call | solution.py:385
  72.3 0.8 %copy.20 = bf16[512,512]{1,0:T(8,128)(2,1)} copy(bf16[512,512]{1,0:T(8,128)(2,1)S(1)} %get-tuple-element.12) | data formatting | bytes 1048576
  73.1 0.8 %copy.21 = bf16[512,512]{1,0:T(8,128)(2,1)} copy(bf16[512,512]{1,0:T(8,128)(2,1)S(1)} %get-tuple-element.13) | data formatting | bytes 1048576
Async XLA Ops:
  4.5 1.0 %copy-start = (bf16[512,512]{1,0:T(8,128)(2,1)S(1)}, bf16[512,512]{1,0:T(8,128)(2,1)}, u32[]{:S(2)}) copy-start(bf16[512,512]{1,0:T(8,128)(2,1)} %q_hbm.1) | copy-start | bytes 1572868
  5.5 1.0 %copy-start.1 = (bf16[512,512]{1,0:T(8,128)(2,1)S(1)}, bf16[512,512]{1,0:T(8,128)(2,1)}, u32[]{:S(2)}) copy-start(bf16[512,512]{1,0:T(8,128)(2,1)} %go_hbm.1) | copy-start | bytes 1572868
  6.6 0.7 copy-start.2

commit v2 on v1

v2 whole, which is shorter than its diff:
```python
import functools

import jax
import jax.numpy as jnp
from jax import lax
from jax.experimental import pallas as pl
from jax.experimental.pallas import tpu as pltpu
from jax.sharding import PartitionSpec as P

MESH = pl.DeviceIdType.MESH
F32 = jnp.float32
BF16 = jnp.bfloat16
TOK = 512
HEAD = 128
HALF = 64
HEADS = 4
ROWS = 128
STEPS = TOK // ROWS
FEAT = 512
NEG = -1e30

NT = (((1,), (1,)), ((), ()))
NN = (((1,), (0,)), ((), ()))
TN = (((0,), (0,)), ((), ()))


def dot(a, b, dims):
    return lax.dot_general(a, b, dims, preferred_element_type=F32)


NUMBER = {}
for name, count in (
    ("kv", 2),
    ("w_turn", 3),
    ("w_y", 6),
    ("w_xh", 8),
    ("w_core", 16),
    ("hid", 8),
    ("part", STEPS),
    ("kg_core", STEPS),
    ("ring_right", 4 * STEPS),
    ("ring_left", 4 * STEPS),
    ("c_y", 6),
    ("c_xh", 1),
    ("b_xl", STEPS),
):
    NUMBER[name] = sum(n for _, n in NUMBER.values()), count
N_REMOTE = sum(n for _, n in NUMBER.values())
LOCAL = {"k": 0, "v": 1, "kw": 2, "vw": 3, "q": 4, "go": 5, "hid": 6, "gq": 14, "gh": 15, "gk": 19, "gv": 20, "mid": 21}
N_LOCAL = 22


def kernel(
    len_ref, hid_hbm, q_hbm, k_hbm, v_hbm, go_hbm, kw_hbm, vw_hbm,
    gq_hbm, gh_hbm, gk_hbm, gv_hbm,
    kv, key_buf, val_buf, q_buf, go_buf, gq_buf,
    w_all, w_mid, hid_buf, dk_acc, dv_acc, part_send, part_got, keep_buf,
    kg_all, kg_other, kg_turned, c_send, c_got, c_own, cx_send, cx_got,
    b_send, b_got, b_own, gh_buf, gk_buf, gv_buf,
    send_sem, recv_sem, local_sem,
):
    dp, tensor = lax.axis_index("dp"), lax.axis_index("tensor")
    core, chip = lax.rem(dp, 2), dp // 2
    xh, y = lax.rem(chip, 2), chip // 2
    xl, z = lax.rem(tensor, 2), tensor // 2

    def at(y=y, xh=xh, core=core, z=z, xl=xl):
        return ((y * 2 + xh) * 2 + core, z * 2 + xl)

    def y_plus(k):
        return lax.rem(y + k, 4)

    def z_plus(k):
        return lax.rem(z + k + 8, 8)

    to_xl, to_core, to_xh = at(xl=1 - xl), at(core=1 - core), at(xh=1 - xh)
    to_right, to_left = at(z=z_plus(1)), at(z=z_plus(-1))
    to_y = [at(y=y_plus(k)) for k in (1, 2, 3)]
    to_y_xh = [at(y=y_plus(k), xh=1 - xh) for k in (1, 2, 3)]
    turn_to = at(y=z // 2, xh=lax.rem(z, 2), z=chip)
    turn_away = chip != z
    ahead, behind = lax.rem(chip + z, 8), lax.rem(chip - z + 8, 8)
    mid_to = at(y=ahead // 2, xh=lax.rem(ahead, 2))
    mid_from = at(y=behind // 2, xh=lax.rem(behind, 2))
    mid_away = z != 0
    rise_to = at(z=behind)
    rise_away = behind != z

    def head_of(part, y, xh):
        return y * 2 + xh if part == 0 else lax.rem(y * 2 + xh - z + 8, 8)

    def local(src, dst, number):
        copy = pltpu.make_async_copy(src, dst, local_sem.at[number])
        copy.start()
        return copy

    started = []

    def remote(src, dst, name, number, device):
        first, count = NUMBER[name]
        assert 0 <= number < count
        copy = pltpu.make_async_remote_copy(
            src_ref=src, dst_ref=dst, send_sem=send_sem.at[first + number],
            recv_sem=recv_sem.at[first + number], device_id=device, device_id_type=MESH,
        )
        return copy

    def send(*args):
        copy = remote(*args)
        copy.start()
        started.append(copy)

    def arrived(dst, name, number):
        first, _ = NUMBER[name]
        pltpu.make_async_remote_copy(
            src_ref=dst, dst_ref=dst, send_sem=send_sem.at[first + number],
            recv_sem=recv_sem.at[first + number], device_id=to_core, device_id_type=MESH,
        ).wait_recv()

    low_half, high_half = pl.ds(0, HALF), pl.ds(HALF, HALF)
    parts = (low_half, high_half)
    barrier = pltpu.get_barrier_semaphore()
    for device in [to_xl, to_core, to_xh, to_right, to_left] + to_y + to_y_xh:
        pl.semaphore_signal(barrier, inc=1, device_id=device, device_id_type=MESH)

    for away, device in ((turn_away, turn_to), (mid_away, mid_from), (rise_away, rise_to)):

        @pl.when(away)
        def _():
            pl.semaphore_signal(barrier, inc=1, device_id=device, device_id_type=MESH)

    in_kv = [
        local(k_hbm, kv.at[0, low_half], LOCAL["k"]),
        local(v_hbm, kv.at[0, high_half], LOCAL["v"]),
    ]
    in_q = local(q_hbm, q_buf, LOCAL["q"])
    in_go = local(go_hbm, go_buf, LOCAL["go"])
    greeted = 11
    for away in (turn_away, mid_away, rise_away):
        greeted = greeted + jnp.where(away, 1, 0)
    pl.semaphore_wait(barrier, greeted)
    send(k_hbm, kv.at[1, low_half], "kv", 0, to_xl)
    send(v_hbm, kv.at[1, high_half], "kv", 1, to_xl)

    moves = []
    for number, (away, device, src, dst, name) in enumerate((
        (turn_away, turn_to, kw_hbm, w_all.at[core, z, low_half], "kw"),
        (mid_away, mid_to, vw_hbm, w_mid, "vw"),
        (rise_away, rise_to, w_mid, w_all.at[core, z, high_half], "mid"),
    )):
        stay = pltpu.make_async_copy(src, dst, local_sem.at[LOCAL[name]])
        moves.append((away, remote(src, dst, "w_turn", number, device), stay))

    def move_start(number):
        away, go, stay = moves[number]
        pl.when(away)(go.start)
        pl.when(jnp.logical_not(away))(stay.start)

    def move_wait(number, dst):
        away, _, stay = moves[number]
        pl.when(away)(lambda: arrived(dst, "w_turn", number))
        pl.when(jnp.logical_not(away))(stay.wait)

    move_start(0)
    move_start(1)
    in_hid = []
    for block in range(8):
        columns = pl.ds(pl.multiple_of((2 * block + core) * FEAT, FEAT), FEAT)
        in_hid.append(local(hid_hbm.at[:, columns], hid_buf.at[block, 0], LOCAL["hid"] + block))
    for block in range(8):
        columns = pl.ds(pl.multiple_of((2 * block + 1 - core) * FEAT, FEAT), FEAT)
        send(hid_hbm.at[:, columns], hid_buf.at[block, 1], "hid", block, to_core)

    lane = lax.broadcasted_iota(jnp.int32, (1, HEADS * ROWS), 1) % ROWS
    bounds, total = [], 0
    for k in range(8):
        total = total + len_ref[0, k]
        bounds.append(total)

    def first_key(rows):
        start = jnp.zeros_like(rows)
        for bound in bounds:
            start = jnp.where(rows >= bound, bound, start)
        return start

    half_lane = lax.broadcasted_iota(jnp.int32, (1, HEAD), 1) < HALF
    lower = xl == 0
    dk_acc[...] = jnp.zeros_like(dk_acc)
    dv_acc[...] = jnp.zeros_like(dv_acc)

    def whole_head(rows):
        own, other = kv[0, rows, :], kv[1, rows, :]
        first, second = jnp.where(lower, own, other), jnp.where(lower, other, own)
        return jnp.concatenate([first, second], axis=0).T

    scale = HEAD ** -0.5
    to_exp2 = scale * 1.4426950408889634

    def heads_of(ref, step):
        return jnp.concatenate(
            [ref[pl.ds(step * ROWS, ROWS), pl.ds(h * HEAD, HEAD)] for h in range(HEADS)], axis=0
        )

    def span(step):
        low = max(0, step - 2) * ROWS
        return low, (step + 1) * ROWS - low

    def softmax(step):
        low, width = span(step)
        rows = lane + step * ROWS
        key_at = low + lax.broadcasted_iota(jnp.int32, (width, HEADS * ROWS), 0)
        allowed = (key_at >= first_key(rows)) & (key_at <= rows)
        scores = dot(key_buf[pl.ds(low, width), :], heads_of(q_buf, step), NT)
        scores = jnp.where(allowed, scores, NEG)
        top = jnp.max(scores, axis=0, keepdims=True)
        expo = jnp.exp2((scores - top) * to_exp2)
        return expo * (1.0 / jnp.sum(expo, axis=0, keepdims=True))

    def gradients(step, probs):
        low, width = span(step)
        seen = pl.ds(low, width)
        queries, grads = heads_of(q_buf, step), heads_of(go_buf, step)
        dprobs = dot(val_buf[seen, :], grads, NT)
        probs_low = probs.astype(BF16)
        delta = jnp.sum(probs_low.astype(F32) * dprobs, axis=0, keepdims=True)
        dscores = (probs * (dprobs - delta) * scale).astype(BF16)
        grad_q = dot(dscores, key_buf[seen, :], TN).astype(BF16)
        for h in range(HEADS):
            gq_buf[pl.ds(step * ROWS, ROWS), pl.ds(h * HEAD, HEAD)] = grad_q[h * ROWS:(h + 1) * ROWS]
        dk_acc[seen, :] += dot(dscores, queries, NN)
        dv_acc[seen, :] += dot(probs_low, grads, NN)

    def part_out(step):
        done = pl.ds(step * ROWS, ROWS)
        dk, dv = dk_acc[done, :], dv_acc[done, :]
        lower_part = jnp.where(half_lane, dk, pltpu.roll(dv, HALF, 1))
        upper_part = jnp.where(half_lane, pltpu.roll(dk, HALF, 1), dv)
        keep_buf[done, :] = jnp.where(lower, lower_part, upper_part)
        part_send[done, :] = jnp.where(lower, upper_part, lower_part).astype(BF16)
        send(part_send.at[done], part_got.at[done], "part", step, to_xl)

    def finish(step):
        done = pl.ds(step * ROWS, ROWS)
        arrived(part_got.at[done], "part", step)
        kg_all[z, done, :] = (keep_buf[done, :] + part_got[done, :].astype(F32)).astype(BF16)

    def ring_hops(step):
        return (4, 3) if step >= 2 else (3, 4)

    def ring_send(step, hop):
        rows = pl.ds(step * ROWS, ROWS)
        right, left = ring_hops(step)
        if hop < right:
            block = kg_all.at[z_plus(-hop), rows]
            send(block, block, "ring_right", step * 4 + hop, to_right)
        if hop < left:
            block = kg_all.at[z_plus(hop), rows]
            send(block, block, "ring_left", step * 4 + hop, to_left)

    def ring_wait(step, hop):
        rows = pl.ds(step * ROWS, ROWS)
        right, left = ring_hops(step)
        if hop < right:
            arrived(kg_all.at[z_plus(-hop - 1), rows], "ring_right", step * 4 + hop)
        if hop < left:
            arrived(kg_all.at[z_plus(hop + 1), rows], "ring_left", step * 4 + hop)

    def kg_start(step):
        rows = pl.ds(step * ROWS, ROWS)
        ring_send(step, 0)
        send(kg_all.at[z, rows], kg_other.at[rows], "kg_core", step, to_core)

    def w_block(part, owner, y, xh):
        return w_all.at[owner, head_of(part, y, xh), parts[part]]

    def w_to_core(ref, part, number):
        send(ref, ref, "w_core", part * 8 + number, to_core)

    def w_enter(part):
        ref = w_block(part, core, y, xh)
        move_wait(2 * part, ref)
        for k in (1, 0, 2):
            send(ref, ref, "w_y", part * 3 + k, to_y[k])
        w_to_core(ref, part, 0)

    def w_across():
        ref = w_block(0, core, y, xh)
        send(ref, ref, "w_xh", 0, to_xh)
        for k in range(3):
            ref = w_block(0, core, y_plus(3 - k), xh)
            arrived(ref, "w_y", k)
            send(ref, ref, "w_xh", k + 1, to_xh)
            w_to_core(ref, 0, k + 1)
        w_enter(1)
        ref = w_block(1, core, y, xh)
        send(ref, ref, "w_xh", 4, to_xh)
        for k in (1, 0, 2):
            send(ref, ref, "w_xh", 5 + k, to_y_xh[k])

    def w_collect():
        for k in range(3):
            ref = w_block(1, core, y_plus(3 - k), xh)
            arrived(ref, "w_y", 3 + k)
            w_to_core(ref, 1, k + 1)
        for part in range(2):
            for k in range(4):
                ref = w_block(part, core, y_plus(4 - k), 1 - xh)
                arrived(ref, "w_xh", part * 4 + k)
                w_to_core(ref, part, 4 + k)

    def w_from_core(part):
        for k in range(4):
            arrived(w_block(part, 1 - core, y_plus(4 - k), xh), "w_core", part * 8 + k)
            arrived(w_block(part, 1 - core, y_plus(4 - k), 1 - xh), "w_core", part * 8 + 4 + k)

    in_kv[0].wait()
    arrived(kv.at[1, low_half], "kv", 0)
    key_buf[...] = whole_head(low_half)
    in_q.wait()
    probs = {step: softmax(step) for step in (3, 2)}
    move_wait(1, w_mid)
    move_start(2)
    in_kv[1].wait()
    arrived(kv.at[1, high_half], "kv", 1)
    val_buf[...] = whole_head(high_half)
    in_go.wait()
    for step in (3, 2):
        gradients(step, probs[step])
    for step in (3, 2):
        part_out(step)
    for step in (1, 0):
        gradients(step, softmax(step))
    for step in (1, 0):
        part_out(step)
    w_enter(0)
    out_gq = local(gq_buf, gq_hbm, LOCAL["gq"])
    for step in (3, 2, 1, 0):
        finish(step)
        kg_start(step)
    w_across()

    def ring_pass(hop, steps=(3, 2, 1, 0)):
        for step in steps:
            ring_wait(step, hop)
            ring_send(step, hop + 1)

    ring_pass(0)

    for block in range(8):
        in_hid[block].wait()
        arrived(hid_buf.at[block, 1], "hid", block)
    for step in (3, 2, 1, 0):
        rows = pl.ds(step * ROWS, ROWS)
        arrived(kg_other.at[rows], "kg_core", step)
    kg_turned[:, pl.ds(0, TOK)] = kg_all[z].T
    kg_turned[:, pl.ds(TOK, TOK)] = kg_other[...].T

    def weight_grad(block):
        hid = hid_buf[block].reshape(2 * TOK, FEAT)
        return dot(kg_turned[...], hid, NN)

    def c_round(kind, x_high):
        for k in (2, 1, 3):
            number = kind * 3 + k - 1
            c_send[number] = weight_grad(y_plus(k) * 2 + x_high).astype(BF16)
            send(c_send.at[number], c_got.at[number], "c_y", number, to_y[k - 1])

    def c_sum(kind):
        total = c_own[kind]
        for k in range(3):
            arrived(c_got.at[kind * 3 + k], "c_y", kind * 3 + k)
            total = total + c_got[kind * 3 + k].astype(F32)
        return total

    c_round(0, 1 - xh)
    ring_pass(1)
    c_round(1, xh)
    ring_pass(2)
    w_collect()
    c_own[0] = weight_grad(y * 2 + 1 - xh)
    c_own[1] = weight_grad(y * 2 + xh)
    w_from_core(0)
    w_from_core(1)

    def all_heads(rows):
        return jnp.concatenate([kg_all[head, rows, :] for head in range(8)], axis=1)

    def features(kind):
        return w_all[kind].reshape(8 * HEAD, FEAT)

    for step in (3, 2, 1, 0):
        rows = pl.ds(step * ROWS, ROWS)
        ring_wait(step, 3)
        b_send[rows, :] = dot(all_heads(rows), features(1 - xl), NN).astype(BF16)
        send(b_send.at[rows], b_got.at[rows], "b_xl", step, to_xl)
        if step == 2:
            cx_send[...] = c_sum(0).astype(BF16)
            send(cx_send, cx_got, "c_xh", 0, to_xh)
    b_own[...] = dot(all_heads(pl.ds(0, TOK)), features(xl), NN)

    mine = c_sum(1)
    arrived(cx_got, "c_xh", 0)
    mine = mine + cx_got[...].astype(F32)
    gk_buf[...] = mine[:HALF]
    gv_buf[...] = mine[HALF:]
    outs = [out_gq, local(gk_buf, gk_hbm, LOCAL["gk"]), local(gv_buf, gv_hbm, LOCAL["gv"])]
    for step in (3, 2, 1, 0):
        rows = pl.ds(step * ROWS, ROWS)
        arrived(b_got.at[rows], "b_xl", step)
        gh_buf[rows, :] = (b_own[rows, :] + b_got[rows, :].astype(F32)).astype(BF16)
        outs.append(local(gh_buf.at[rows], gh_hbm.at[rows], LOCAL["gh"] + step))
    for copy in outs:
        copy.wait()
    for copy in started:
        copy.wait_send()

    for away, go, _ in moves:
        pl.when(away)(go.wait_send)


def hand_over(*refs):
    for n in range(4):
        refs[4 + n][...] = refs[n][...]


def body(hidden, query, keys, values, grad_out, key_weight, value_weight, lengths):
    anywhere = pl.BlockSpec(memory_space=pl.ANY)

    def vmem(*shape, dtype=BF16):
        return pltpu.VMEM(shape, dtype)

    results = pl.pallas_call(
        kernel,
        out_shape=(
            jax.ShapeDtypeStruct((TOK, HEADS * HEAD), BF16),
            jax.ShapeDtypeStruct((TOK, FEAT), BF16),
            jax.ShapeDtypeStruct((HALF, FEAT), F32),
            jax.ShapeDtypeStruct((HALF, FEAT), F32),
        ),
        in_specs=[pl.BlockSpec(memory_space=pltpu.SMEM)] + [pl.BlockSpec(memory_space=pltpu.HBM)] * 7,
        out_specs=(anywhere,) * 4,
        scratch_shapes=[
            vmem(2, HEAD, TOK), vmem(TOK, HEAD), vmem(TOK, HEAD),
            vmem(TOK, HEADS * HEAD), vmem(TOK, HEADS * HEAD), vmem(TOK, HEADS * HEAD),
            vmem(2, 8, HEAD, FEAT), vmem(HALF, FEAT), vmem(8, 2, TOK, FEAT),
            vmem(TOK, HEAD, dtype=F32), vmem(TOK, HEAD, dtype=F32),
            vmem(TOK, HEAD), vmem(TOK, HEAD), vmem(TOK, HEAD, dtype=F32),
            vmem(8, TOK, HEAD), vmem(TOK, HEAD), vmem(HEAD, 2 * TOK),
            vmem(6, HEAD, FEAT), vmem(6, HEAD, FEAT), vmem(2, HEAD, FEAT, dtype=F32),
            vmem(HEAD, FEAT), vmem(HEAD, FEAT),
            vmem(TOK, FEAT), vmem(TOK, FEAT), vmem(TOK, FEAT, dtype=F32), vmem(TOK, FEAT),
            vmem(HALF, FEAT, dtype=F32), vmem(HALF, FEAT, dtype=F32),
            pltpu.SemaphoreType.DMA((N_REMOTE,)), pltpu.SemaphoreType.DMA((N_REMOTE,)),
            pltpu.SemaphoreType.DMA((N_LOCAL,)),
        ],
        compiler_params=pltpu.CompilerParams(
            collective_id=0, has_side_effects=True, vmem_limit_bytes=58 * 1024 * 1024
        ),
        name="attention_backward",
    )(lengths, hidden, query, keys.T, values.T, grad_out, key_weight.T, value_weight.T)
    grad_query, grad_hidden, key_turned, value_turned = pl.pallas_call(
        hand_over,
        out_shape=tuple(jax.ShapeDtypeStruct(r.shape, r.dtype) for r in results),
        compiler_params=pltpu.CompilerParams(vmem_limit_bytes=58 * 1024 * 1024),
        name="hand_over",
    )(*results)
    return grad_query, grad_hidden, key_turned.T, value_turned.T


def solution(mesh):
    placed = (
        P("dp", None),
        P("dp", "tensor"),
        P("dp", "tensor"),
        P("dp", "tensor"),
        P("dp", "tensor"),
        P("dp", "tensor"),
        P("dp", "tensor"),
        P("dp", None),
    )
    return jax.shard_map(
        body,
        mesh=mesh,
        in_specs=placed,
        out_specs=(P("dp", "tensor"), P("dp", "tensor"), P("dp", "tensor"), P("dp", "tensor")),
        check_vma=False,
    )
```

time: 74.3 us -> 61.8 us (0.83)
  the two profiles are of different devices: /device:TPU:32 before, /device:TPU:9 now
where the time goes in v2:
time: 61.8 us; the launch traced here: 61.7 us
  Pallas kernels  61 us (99%)
  between operations  0.64 us (1%)
    pallas_call x1, Pallas kernels, body(): pl.pallas_call(kernel, out_shape=(jax.ShapeDtypeStruct((TOK, HEADS * HEAD...  58.7 us
    pallas_call x1, Pallas kernels, body(): pl.pallas_call(hand_over, out_shape=tuple((jax.ShapeDtypeStruct(r.shape,...  2.34 us

profile of v2, /device:TPU:9, one launch (start us, length us, event | category | flops | bytes accessed | tf_op | source)
XLA Modules:
  0.0 61.7 jit_solution(12423344757952790576)
XLA Ops:
  0.6 58.7 %attention_backward.1 = (bf16[512,512]{1,0:T(8,128)(2,1)}, bf16[512,512]{1,0:T(8,128)(2,1)}, f32[64,512]{1,0:T(8,128)}, f32[64,512]{1,0:T(8,128)}) custom-call(s32[1,8]{1,0:T(1,128)} %len_ref.1, bf16[512,8192]{1,0:T(8,128)(2,1)} %hid_hbm.1, bf16[512,512]{1,0:T(8,128)(2,1)} %q_hbm.1, bf16[64,512]{1,0:T(8,128)(2,1)} %bitcast.6, bf16[64,512]{1,0:T(8,128)(2,1)} %bitcast.7, ...), custom_call_target="tpu_custom_call" | custom-call | tf_op jit(solution)/shard_map/attention_backward/pallas_call | solution.py:432
  59.3 2.3 %hand_over.1 = (bf16[512,512]{1,0:T(8,128)(2,1)}, bf16[512,512]{1,0:T(8,128)(2,1)}, f32[64,512]{1,0:T(8,128)}, f32[64,512]{1,0:T(8,128)}) custom-call(bf16[512,512]{1,0:T(8,128)(2,1)} %get-tuple-element.12.refs_0_, bf16[512,512]{1,0:T(8,128)(2,1)} %get-tuple-element.13.refs_1_, f32[64,512]{1,0:T(8,128)} %get-tuple-element.14.refs_2_, ...), custom_call_target="tpu_custom_call" | custom-call | tf_op jit(solution)/shard_map/hand_over/pallas_call | solution.py:461

commit v3 on v2

--- a/solution.py
+++ b/solution.py
@@ -33,8 +33,8 @@
     ("kv", 2),
     ("w_turn", 3),
     ("w_y", 6),
-    ("w_xh", 8),
-    ("w_core", 16),
+    ("w_xh", 1),
+    ("w_core", 8),
     ("hid", 8),
     ("part", STEPS),
     ("kg_core", STEPS),
@@ -42,22 +42,22 @@
     ("ring_left", 4 * STEPS),
     ("c_y", 6),
     ("c_xh", 1),
-    ("b_xl", STEPS),
+    ("kg_xl", 8 * STEPS),
 ):
     NUMBER[name] = sum(n for _, n in NUMBER.values()), count
 N_REMOTE = sum(n for _, n in NUMBER.values())
-LOCAL = {"k": 0, "v": 1, "kw": 2, "vw": 3, "q": 4, "go": 5, "hid": 6, "gq": 14, "gh": 15, "gk": 19, "gv": 20, "mid": 21}
-N_LOCAL = 22
+LOCAL = {"k": 0, "v": 1, "kw": 2, "vw": 3, "q": 4, "go": 5, "hid": 6, "gq": 14, "gh": 15, "gk": 19, "gv": 20, "len": 21, "mid": 22}
+N_LOCAL = 23
 
 
 def kernel(
-    len_ref, hid_hbm, q_hbm, k_hbm, v_hbm, go_hbm, kw_hbm, vw_hbm,
+    len_hbm, hid_hbm, q_hbm, k_hbm, v_hbm, go_hbm, kw_hbm, vw_hbm,
     gq_hbm, gh_hbm, gk_hbm, gv_hbm,
     kv, key_buf, val_buf, q_buf, go_buf, gq_buf,
     w_all, w_mid, hid_buf, dk_acc, dv_acc, part_send, part_got, keep_buf,
     kg_all, kg_other, kg_turned, c_send, c_got, c_own, cx_send, cx_got,
-    b_send, b_got, b_own, gh_buf, gk_buf, gv_buf,
-    send_sem, recv_sem, local_sem,
+    b_own, gh_buf, gk_buf, gv_buf,
+    len_ref, send_sem, recv_sem, local_sem,
 ):
     dp, tensor = lax.axis_index("dp"), lax.axis_index("tensor")
     core, chip = lax.rem(dp, 2), dp // 2
@@ -76,18 +76,15 @@
     to_xl, to_core, to_xh = at(xl=1 - xl), at(core=1 - core), at(xh=1 - xh)
     to_right, to_left = at(z=z_plus(1)), at(z=z_plus(-1))
     to_y = [at(y=y_plus(k)) for k in (1, 2, 3)]
-    to_y_xh = [at(y=y_plus(k), xh=1 - xh) for k in (1, 2, 3)]
-    turn_to = at(y=z // 2, xh=lax.rem(z, 2), z=chip)
-    turn_away = chip != z
     ahead, behind = lax.rem(chip + z, 8), lax.rem(chip - z + 8, 8)
     mid_to = at(y=ahead // 2, xh=lax.rem(ahead, 2))
     mid_from = at(y=behind // 2, xh=lax.rem(behind, 2))
     mid_away = z != 0
-    rise_to = at(z=behind)
-    rise_away = behind != z
-
-    def head_of(part, y, xh):
-        return y * 2 + xh if part == 0 else lax.rem(y * 2 + xh - z + 8, 8)
+    rise_to = at(z=behind, core=xl, xl=core)
+    rise_away = (behind != z) | (core != xl)
+
+    def head_of(y, xh):
+        return lax.rem(y * 2 + xh - z + 8, 8)
 
     def local(src, dst, number):
         copy = pltpu.make_async_copy(src, dst, local_sem.at[number])
@@ -120,10 +117,10 @@
     low_half, high_half = pl.ds(0, HALF), pl.ds(HALF, HALF)
     parts = (low_half, high_half)
     barrier = pltpu.get_barrier_semaphore()
-    for device in [to_xl, to_core, to_xh, to_right, to_left] + to_y + to_y_xh:
+    for device in [to_xl, to_core, to_xh, to_right, to_left] + to_y:
         pl.semaphore_signal(barrier, inc=1, device_id=device, device_id_type=MESH)
 
-    for away, device in ((turn_away, turn_to), (mid_away, mid_from), (rise_away, rise_to)):
+    for away, device in ((mid_away, mid_from), (rise_away, rise_to)):
 
         @pl.when(away)
         def _():
@@ -133,20 +130,18 @@
         local(k_hbm, kv.at[0, low_half], LOCAL["k"]),
         local(v_hbm, kv.at[0, high_half], LOCAL["v"]),
     ]
+    in_len = local(len_hbm, len_ref, LOCAL["len"])
     in_q = local(q_hbm, q_buf, LOCAL["q"])
     in_go = local(go_hbm, go_buf, LOCAL["go"])
-    greeted = 11
-    for away in (turn_away, mid_away, rise_away):
-        greeted = greeted + jnp.where(away, 1, 0)
-    pl.semaphore_wait(barrier, greeted)
+    pl.semaphore_wait(barrier, 8 + jnp.where(mid_away, 1, 0) + jnp.where(rise_away, 1, 0))
     send(k_hbm, kv.at[1, low_half], "kv", 0, to_xl)
     send(v_hbm, kv.at[1, high_half], "kv", 1, to_xl)
 
     moves = []
     for number, (away, device, src, dst, name) in enumerate((
-        (turn_away, turn_to, kw_hbm, w_all.at[core, z, low_half], "kw"),
-        (mid_away, mid_to, vw_hbm, w_mid, "vw"),
-        (rise_away, rise_to, w_mid, w_all.at[core, z, high_half], "mid"),
+        (mid_away, mid_to, kw_hbm, w_mid.at[low_half], "kw"),
+        (mid_away, mid_to, vw_hbm, w_mid.at[high_half], "vw"),
+        (rise_away, rise_to, w_mid, w_all.at[xl, z], "mid"),
     )):
         stay = pltpu.make_async_copy(src, dst, local_sem.at[LOCAL[name]])
         moves.append((away, remote(src, dst, "w_turn", number, device), stay))
@@ -161,8 +156,6 @@
         pl.when(away)(lambda: arrived(dst, "w_turn", number))
         pl.when(jnp.logical_not(away))(stay.wait)
 
-    move_start(0)
-    move_start(1)
     in_hid = []
     for block in range(8):
         columns = pl.ds(pl.multiple_of((2 * block + core) * FEAT, FEAT), FEAT)
@@ -171,6 +164,7 @@
         columns = pl.ds(pl.multiple_of((2 * block + 1 - core) * FEAT, FEAT), FEAT)
         send(hid_hbm.at[:, columns], hid_buf.at[block, 1], "hid", block, to_core)
 
+    in_len.wait()
     lane = lax.broadcasted_iota(jnp.int32, (1, HEADS * ROWS), 1) % ROWS
     bounds, total = [], 0
     for k in range(8):
@@ -242,7 +236,7 @@
     def finish(step):
         done = pl.ds(step * ROWS, ROWS)
         arrived(part_got.at[done], "part", step)
-        kg_all[z, done, :] = (keep_buf[done, :] + part_got[done, :].astype(F32)).astype(BF16)
+        kg_all[0, z, done, :] = (keep_buf[done, :] + part_got[done, :].astype(F32)).astype(BF16)
 
     def ring_hops(step):
         return (4, 3) if step >= 2 else (3, 4)
@@ -251,77 +245,70 @@
         rows = pl.ds(step * ROWS, ROWS)
         right, left = ring_hops(step)
         if hop < right:
-            block = kg_all.at[z_plus(-hop), rows]
+            block = kg_all.at[0, z_plus(-hop), rows]
             send(block, block, "ring_right", step * 4 + hop, to_right)
         if hop < left:
-            block = kg_all.at[z_plus(hop), rows]
+            block = kg_all.at[0, z_plus(hop), rows]
             send(block, block, "ring_left", step * 4 + hop, to_left)
 
     def ring_wait(step, hop):
         rows = pl.ds(step * ROWS, ROWS)
         right, left = ring_hops(step)
         if hop < right:
-            arrived(kg_all.at[z_plus(-hop - 1), rows], "ring_right", step * 4 + hop)
+            arrived(kg_all.at[0, z_plus(-hop - 1), rows], "ring_right", step * 4 + hop)
         if hop < left:
-            arrived(kg_all.at[z_plus(hop + 1), rows], "ring_left", step * 4 + hop)
+            arrived(kg_all.at[0, z_plus(hop + 1), rows], "ring_left", step * 4 + hop)
+
+    def across(step, number):
+        head = z_plus((number + 1) // 2 * (1 if number % 2 else -1))
+        rows = pl.ds(step * ROWS, ROWS)
+        send(kg_all.at[0, head, rows], kg_all.at[1, head, rows], "kg_xl", step * 8 + number, to_xl)
 
     def kg_start(step):
         rows = pl.ds(step * ROWS, ROWS)
         ring_send(step, 0)
-        send(kg_all.at[z, rows], kg_other.at[rows], "kg_core", step, to_core)
-
-    def w_block(part, owner, y, xh):
-        return w_all.at[owner, head_of(part, y, xh), parts[part]]
-
-    def w_to_core(ref, part, number):
-        send(ref, ref, "w_core", part * 8 + number, to_core)
-
-    def w_enter(part):
-        ref = w_block(part, core, y, xh)
-        move_wait(2 * part, ref)
+        across(step, 0)
+        send(kg_all.at[0, z, rows], kg_other.at[rows], "kg_core", step, to_core)
+
+    def w_block(owner, y, xh):
+        return w_all.at[owner, head_of(y, xh)]
+
+    def w_on(number, x_high):
+        ref = w_block(core, y, x_high)
         for k in (1, 0, 2):
-            send(ref, ref, "w_y", part * 3 + k, to_y[k])
-        w_to_core(ref, part, 0)
-
-    def w_across():
-        ref = w_block(0, core, y, xh)
+            send(ref, ref, "w_y", number * 3 + k, to_y[k])
+        send(ref, ref, "w_core", number * 4, to_core)
+
+    def w_enter():
+        ref = w_block(core, y, xh)
+        move_wait(2, ref)
         send(ref, ref, "w_xh", 0, to_xh)
+        w_on(0, xh)
+
+    def w_other_xh():
+        arrived(w_block(core, y, 1 - xh), "w_xh", 0)
+        w_on(1, 1 - xh)
+
+    def w_from_y(number, x_high):
         for k in range(3):
-            ref = w_block(0, core, y_plus(3 - k), xh)
-            arrived(ref, "w_y", k)
-            send(ref, ref, "w_xh", k + 1, to_xh)
-            w_to_core(ref, 0, k + 1)
-        w_enter(1)
-        ref = w_block(1, core, y, xh)
-        send(ref, ref, "w_xh", 4, to_xh)
-        for k in (1, 0, 2):
-            send(ref, ref, "w_xh", 5 + k, to_y_xh[k])
-
-    def w_collect():
-        for k in range(3):
-            ref = w_block(1, core, y_plus(3 - k), xh)
-            arrived(ref, "w_y", 3 + k)
-            w_to_core(ref, 1, k + 1)
-        for part in range(2):
+            ref = w_block(core, y_plus(3 - k), x_high)
+            arrived(ref, "w_y", number * 3 + k)
+            send(ref, ref, "w_core", number * 4 + k + 1, to_core)
+
+    def w_from_core():
+        for number, x_high in ((0, xh), (1, 1 - xh)):
             for k in range(4):
-                ref = w_block(part, core, y_plus(4 - k), 1 - xh)
-                arrived(ref, "w_xh", part * 4 + k)
-                w_to_core(ref, part, 4 + k)
-
-    def w_from_core(part):
-        for k in range(4):
-            arrived(w_block(part, 1 - core, y_plus(4 - k), xh), "w_core", part * 8 + k)
-            arrived(w_block(part, 1 - core, y_plus(4 - k), 1 - xh), "w_core", part * 8 + 4 + k)
+                arrived(w_block(1 - core, y_plus(4 - k), x_high), "w_core", number * 4 + k)
 
     in_kv[0].wait()
     arrived(kv.at[1, low_half], "kv", 0)
     key_buf[...] = whole_head(low_half)
     in_q.wait()
     probs = {step: softmax(step) for step in (3, 2)}
-    move_wait(1, w_mid)
-    move_start(2)
     in_kv[1].wait()
     arrived(kv.at[1, high_half], "kv", 1)
+    move_start(0)
+    move_start(1)
     val_buf[...] = whole_head(high_half)
     in_go.wait()
     for step in (3, 2):
@@ -332,19 +319,26 @@
         gradients(step, softmax(step))
     for step in (1, 0):
         part_out(step)
-    w_enter(0)
     out_gq = local(gq_buf, gq_hbm, LOCAL["gq"])
     for step in (3, 2, 1, 0):
+        if step == 1:
+            for number, rows in enumerate(parts):
+                move_wait(number, w_mid.at[rows])
+            move_start(2)
         finish(step)
         kg_start(step)
-    w_across()
 
     def ring_pass(hop, steps=(3, 2, 1, 0)):
         for step in steps:
             ring_wait(step, hop)
-            ring_send(step, hop + 1)
-
-    ring_pass(0)
+            if hop < 3:
+                ring_send(step, hop + 1)
+            right, left = ring_hops(step)
+            if hop < left:
+                across(step, 2 * hop + 1)
+            if hop < right:
+                across(step, 2 * hop + 2 if hop < 3 else 7)
+
 
     for block in range(8):
         in_hid[block].wait()
@@ -352,7 +346,7 @@
     for step in (3, 2, 1, 0):
         rows = pl.ds(step * ROWS, ROWS)
         arrived(kg_other.at[rows], "kg_core", step)
-    kg_turned[:, pl.ds(0, TOK)] = kg_all[z].T
+    kg_turned[:, pl.ds(0, TOK)] = kg_all[0, z].T
     kg_turned[:, pl.ds(TOK, TOK)] = kg_other[...].T
 
     def weight_grad(block):
@@ -373,42 +367,44 @@
         return total
 
     c_round(0, 1 - xh)
+    ring_pass(0)
+    w_enter()
+    c_round(1, xh)
     ring_pass(1)
-    c_round(1, xh)
-    ring_pass(2)
-    w_collect()
     c_own[0] = weight_grad(y * 2 + 1 - xh)
     c_own[1] = weight_grad(y * 2 + xh)
-    w_from_core(0)
-    w_from_core(1)
-
-    def all_heads(rows):
-        return jnp.concatenate([kg_all[head, rows, :] for head in range(8)], axis=1)
+    w_other_xh()
+    ring_pass(2)
+    cx_send[...] = c_sum(0).astype(BF16)
+    send(cx_send, cx_got, "c_xh", 0, to_xh)
+    ring_pass(3)
+    w_from_y(0, xh)
+    mine = c_sum(1)
+    w_from_y(1, 1 - xh)
+    w_from_core()
+
+    def all_heads(line, rows):
+        return jnp.concatenate([kg_all[line, head, rows, :] for head in range(8)], axis=1)
 
     def features(kind):
         return w_all[kind].reshape(8 * HEAD, FEAT)
 
+    b_own[...] = dot(all_heads(0, pl.ds(0, TOK)), features(xl), NN)
+    outs = [out_gq]
     for step in (3, 2, 1, 0):
         rows = pl.ds(step * ROWS, ROWS)
-        ring_wait(step, 3)
-        b_send[rows, :] = dot(all_heads(rows), features(1 - xl), NN).astype(BF16)
-        send(b_send.at[rows], b_got.at[rows], "b_xl", step, to_xl)
-        if step == 2:
-            cx_send[...] = c_sum(0).astype(BF16)
-            send(cx_send, cx_got, "c_xh", 0, to_xh)
-    b_own[...] = dot(all_heads(pl.ds(0, TOK)), features(xl), NN)
-
-    mine = c_sum(1)
-    arrived(cx_got, "c_xh", 0)
-    mine = mine + cx_got[...].astype(F32)
-    gk_buf[...] = mine[:HALF]
-    gv_buf[...] = mine[HALF:]
-    outs = [out_gq, local(gk_buf, gk_hbm, LOCAL["gk"]), local(gv_buf, gv_hbm, LOCAL["gv"])]
-    for step in (3, 2, 1, 0):
-        rows = pl.ds(step * ROWS, ROWS)
-        arrived(b_got.at[rows], "b_xl", step)
-        gh_buf[rows, :] = (b_own[rows, :] + b_got[rows, :].astype(F32)).astype(BF16)
+        for number in range(8):
+            head = z_plus((number + 1) // 2 * (1 if number % 2 else -1))
+            arrived(kg_all.at[1, head, rows], "kg_xl", step * 8 + number)
+        gh_buf[rows, :] = (b_own[rows, :] + dot(all_heads(1, rows), features(1 - xl), NN)).astype(BF16)
         outs.append(local(gh_buf.at[rows], gh_hbm.at[rows], LOCAL["gh"] + step))
+        if step == 1:
+            arrived(cx_got, "c_xh", 0)
+            mine = mine + cx_got[...].astype(F32)
+            gk_buf[...] = mine[:HALF]
+            gv_buf[...] = mine[HALF:]
+            outs.append(local(gk_buf, gk_hbm, LOCAL["gk"]))
+            outs.append(local(gv_buf, gv_hbm, LOCAL["gv"]))
     for copy in outs:
         copy.wait()
     for copy in started:
@@ -419,8 +415,16 @@
 
 
 def hand_over(*refs):
-    for n in range(4):
-        refs[4 + n][...] = refs[n][...]
+    srcs, dsts, bufs, sems = refs[:4], refs[4:8], refs[8:12], refs[12]
+    ins = [pltpu.make_async_copy(srcs[n], bufs[n], sems.at[n]) for n in range(4)]
+    outs = [pltpu.make_async_copy(bufs[n], dsts[n], sems.at[4 + n]) for n in range(4)]
+    for copy in ins:
+        copy.start()
+    for arriving, leaving in zip(ins, outs):
+        arriving.wait()
+        leaving.start()
+    for copy in outs:
+        copy.wait()
 
 
 def body(hidden, query, keys, values, grad_out, key_weight, value_weight, lengths):
@@ -437,19 +441,20 @@
             jax.ShapeDtypeStruct((HALF, FEAT), F32),
             jax.ShapeDtypeStruct((HALF, FEAT), F32),
         ),
-        in_specs=[pl.BlockSpec(memory_space=pltpu.SMEM)] + [pl.BlockSpec(memory_space=pltpu.HBM)] * 7,
+        in_specs=[pl.BlockSpec(memory_space=pltpu.HBM)] * 8,
         out_specs=(anywhere,) * 4,
         scratch_shapes=[
             vmem(2, HEAD, TOK), vmem(TOK, HEAD), vmem(TOK, HEAD),
             vmem(TOK, HEADS * HEAD), vmem(TOK, HEADS * HEAD), vmem(TOK, HEADS * HEAD),
-            vmem(2, 8, HEAD, FEAT), vmem(HALF, FEAT), vmem(8, 2, TOK, FEAT),
+            vmem(2, 8, HEAD, FEAT), vmem(HEAD, FEAT), vmem(8, 2, TOK, FEAT),
             vmem(TOK, HEAD, dtype=F32), vmem(TOK, HEAD, dtype=F32),
             vmem(TOK, HEAD), vmem(TOK, HEAD), vmem(TOK, HEAD, dtype=F32),
-            vmem(8, TOK, HEAD), vmem(TOK, HEAD), vmem(HEAD, 2 * TOK),
+            vmem(2, 8, TOK, HEAD), vmem(TOK, HEAD), vmem(HEAD, 2 * TOK),
             vmem(6, HEAD, FEAT), vmem(6, HEAD, FEAT), vmem(2, HEAD, FEAT, dtype=F32),
             vmem(HEAD, FEAT), vmem(HEAD, FEAT),
-            vmem(TOK, FEAT), vmem(TOK, FEAT), vmem(TOK, FEAT, dtype=F32), vmem(TOK, FEAT),
+            vmem(TOK, FEAT, dtype=F32), vmem(TOK, FEAT),
             vmem(HALF, FEAT, dtype=F32), vmem(HALF, FEAT, dtype=F32),
+            pltpu.SMEM((1, 8), jnp.int32),
             pltpu.SemaphoreType.DMA((N_REMOTE,)), pltpu.SemaphoreType.DMA((N_REMOTE,)),
             pltpu.SemaphoreType.DMA((N_LOCAL,)),
         ],
@@ -461,6 +466,9 @@
     grad_query, grad_hidden, key_turned, value_turned = pl.pallas_call(
         hand_over,
         out_shape=tuple(jax.ShapeDtypeStruct(r.shape, r.dtype) for r in results),
+        in_specs=[anywhere] * 4,
+        out_specs=(anywhere,) * 4,
+        scratch_shapes=[vmem(*r.shape, dtype=r.dtype) for r in results] + [pltpu.SemaphoreType.DMA((8,))],
         compiler_params=pltpu.CompilerParams(vmem_limit_bytes=58 * 1024 * 1024),
         name="hand_over",
     )(*results)

time: 61.8 us -> 57.6 us (0.932)
  the two profiles are of different devices: /device:TPU:9 before, /device:TPU:32 now
where the time goes in v3:
time: 57.6 us; the launch traced here: 56.9 us
  Pallas kernels  56.3 us (98%)
  between operations  0.64 us (1%)
    pallas_call x1, Pallas kernels, body(): pl.pallas_call(kernel, out_shape=(jax.ShapeDtypeStruct((TOK, HEADS * HEAD...  54.1 us
    pallas_call x1, Pallas kernels, body(): pl.pallas_call(hand_over, out_shape=tuple((jax.ShapeDtypeStruct(r.shape,...  2.16 us

profile of v3, /device:TPU:32, one launch (start us, length us, event | category | flops | bytes accessed | tf_op | source)
XLA Modules:
  0.0 56.9 jit_solution(12141258062100368810)
XLA Ops:
  0.6 54.1 %attention_backward.1 = (bf16[512,512]{1,0:T(8,128)(2,1)}, bf16[512,512]{1,0:T(8,128)(2,1)}, f32[64,512]{1,0:T(8,128)}, f32[64,512]{1,0:T(8,128)}) custom-call(s32[1,8]{1,0:T(1,128)} %len_hbm.1, bf16[512,8192]{1,0:T(8,128)(2,1)} %hid_hbm.1, bf16[512,512]{1,0:T(8,128)(2,1)} %q_hbm.1, bf16[64,512]{1,0:T(8,128)(2,1)} %bitcast.6, bf16[64,512]{1,0:T(8,128)(2,1)} %bitcast.7, ...), custom_call_target="tpu_custom_call" | custom-call | tf_op jit(solution)/shard_map/attention_backward/pallas_call | solution.py:436
  54.8 2.2 %hand_over.1 = (bf16[512,512]{1,0:T(8,128)(2,1)}, bf16[512,512]{1,0:T(8,128)(2,1)}, f32[64,512]{1,0:T(8,128)}, f32[64,512]{1,0:T(8,128)}) custom-call(bf16[512,512]{1,0:T(8,128)(2,1)} %get-tuple-element.12.refs_0_, bf16[512,512]{1,0:T(8,128)(2,1)} %get-tuple-element.13.refs_1_, f32[64,512]{1,0:T(8,128)} %get-tuple-element.14.refs_2_, ...), custom_call_target="tpu_custom_call" | custom-call | tf_op jit(solution)/shard_map/hand_over/pallas_call | solution.py:466

commit v4 on v3

--- a/solution.py
+++ b/solution.py
@@ -303,12 +303,12 @@
     in_kv[0].wait()
     arrived(kv.at[1, low_half], "kv", 0)
     key_buf[...] = whole_head(low_half)
+    move_start(0)
+    move_start(1)
     in_q.wait()
     probs = {step: softmax(step) for step in (3, 2)}
     in_kv[1].wait()
     arrived(kv.at[1, high_half], "kv", 1)
-    move_start(0)
-    move_start(1)
     val_buf[...] = whole_head(high_half)
     in_go.wait()
     for step in (3, 2):
@@ -320,11 +320,10 @@
     for step in (1, 0):
         part_out(step)
     out_gq = local(gq_buf, gq_hbm, LOCAL["gq"])
+    for number, rows in enumerate(parts):
+        move_wait(number, w_mid.at[rows])
+    move_start(2)
     for step in (3, 2, 1, 0):
-        if step == 1:
-            for number, rows in enumerate(parts):
-                move_wait(number, w_mid.at[rows])
-            move_start(2)
         finish(step)
         kg_start(step)
 
@@ -367,8 +366,9 @@
         return total
 
     c_round(0, 1 - xh)
-    ring_pass(0)
+    ring_pass(0, (3, 2))
     w_enter()
+    ring_pass(0, (1, 0))
     c_round(1, xh)
     ring_pass(1)
     c_own[0] = weight_grad(y * 2 + 1 - xh)
@@ -381,7 +381,6 @@
     w_from_y(0, xh)
     mine = c_sum(1)
     w_from_y(1, 1 - xh)
-    w_from_core()
 
     def all_heads(line, rows):
         return jnp.concatenate([kg_all[line, head, rows, :] for head in range(8)], axis=1)
@@ -389,14 +388,19 @@
     def features(kind):
         return w_all[kind].reshape(8 * HEAD, FEAT)
 
-    b_own[...] = dot(all_heads(0, pl.ds(0, TOK)), features(xl), NN)
-    outs = [out_gq]
     for step in (3, 2, 1, 0):
         rows = pl.ds(step * ROWS, ROWS)
         for number in range(8):
             head = z_plus((number + 1) // 2 * (1 if number % 2 else -1))
             arrived(kg_all.at[1, head, rows], "kg_xl", step * 8 + number)
-        gh_buf[rows, :] = (b_own[rows, :] + dot(all_heads(1, rows), features(1 - xl), NN)).astype(BF16)
+    first_line = jnp.where(core == xl, 0, 1)
+    b_own[...] = dot(all_heads(first_line, pl.ds(0, TOK)), features(core), NN)
+    w_from_core()
+    outs = [out_gq]
+    for step in (3, 2, 1, 0):
+        rows = pl.ds(step * ROWS, ROWS)
+        rest = dot(all_heads(1 - first_line, rows), features(1 - core), NN)
+        gh_buf[rows, :] = (b_own[rows, :] + rest).astype(BF16)
         outs.append(local(gh_buf.at[rows], gh_hbm.at[rows], LOCAL["gh"] + step))
         if step == 1:
             arrived(cx_got, "c_xh", 0)

time: 57.6 us -> 58.4 us (1.014)
  Pallas kernels: 56.3 us -> 57 us
    pallas_call x1, Pallas kernels: 54.1 us -> 54.8 us  [body(): pl.pallas_call(kernel, out_shape=(jax.ShapeDtypeStruct((TOK, HEADS * HEAD...]
where the time goes in v4:
time: 58.4 us; the launch traced here: 57.6 us
  Pallas kernels  57 us (98%)
  between operations  0.64 us (1%)
    pallas_call x1, Pallas kernels, body(): pl.pallas_call(kernel, out_shape=(jax.ShapeDtypeStruct((TOK, HEADS * HEAD...  54.8 us
    pallas_call x1, Pallas kernels, body(): pl.pallas_call(hand_over, out_shape=tuple((jax.ShapeDtypeStruct(r.shape,...  2.16 us

profile of v4, /device:TPU:32, one launch (start us, length us, event | category | flops | bytes accessed | tf_op | source)
XLA Modules:
  0.0 57.6 jit_solution(3147638979655300677)
XLA Ops:
  0.6 54.8 %attention_backward.1 = (bf16[512,512]{1,0:T(8,128)(2,1)}, bf16[512,512]{1,0:T(8,128)(2,1)}, f32[64,512]{1,0:T(8,128)}, f32[64,512]{1,0:T(8,128)}) custom-call(s32[1,8]{1,0:T(1,128)} %len_hbm.1, bf16[512,8192]{1,0:T(8,128)(2,1)} %hid_hbm.1, bf16[512,512]{1,0:T(8,128)(2,1)} %q_hbm.1, bf16[64,512]{1,0:T(8,128)(2,1)} %bitcast.6, bf16[64,512]{1,0:T(8,128)(2,1)} %bitcast.7, ...), custom_call_target="tpu_custom_call" | custom-call | tf_op jit(solution)/shard_map/attention_backward/pallas_call | solution.py:440
  55.5 2.2 %hand_over.1 = (bf16[512,512]{1,0:T(8,128)(2,1)}, bf16[512,512]{1,0:T(8,128)(2,1)}, f32[64,512]{1,0:T(8,128)}, f32[64,512]{1,0:T(8,128)}) custom-call(bf16[512,512]{1,0:T(8,128)(2,1)} %get-tuple-element.12.refs_0_, bf16[512,512]{1,0:T(8,128)(2,1)} %get-tuple-element.13.refs_1_, f32[64,512]{1,0:T(8,128)} %get-tuple-element.14.refs_2_, ...), custom_call_target="tpu_custom_call" | custom-call | tf_op jit(solution)/shard_map/hand_over/pallas_call | solution.py:470

commit v5 on v4

--- a/solution.py
+++ b/solution.py
@@ -381,6 +381,7 @@
     w_from_y(0, xh)
     mine = c_sum(1)
     w_from_y(1, 1 - xh)
+    w_from_core()
 
     def all_heads(line, rows):
         return jnp.concatenate([kg_all[line, head, rows, :] for head in range(8)], axis=1)
@@ -388,19 +389,14 @@
     def features(kind):
         return w_all[kind].reshape(8 * HEAD, FEAT)
 
+    b_own[...] = dot(all_heads(0, pl.ds(0, TOK)), features(xl), NN)
+    outs = [out_gq]
     for step in (3, 2, 1, 0):
         rows = pl.ds(step * ROWS, ROWS)
         for number in range(8):
             head = z_plus((number + 1) // 2 * (1 if number % 2 else -1))
             arrived(kg_all.at[1, head, rows], "kg_xl", step * 8 + number)
-    first_line = jnp.where(core == xl, 0, 1)
-    b_own[...] = dot(all_heads(first_line, pl.ds(0, TOK)), features(core), NN)
-    w_from_core()
-    outs = [out_gq]
-    for step in (3, 2, 1, 0):
-        rows = pl.ds(step * ROWS, ROWS)
-        rest = dot(all_heads(1 - first_line, rows), features(1 - core), NN)
-        gh_buf[rows, :] = (b_own[rows, :] + rest).astype(BF16)
+        gh_buf[rows, :] = (b_own[rows, :] + dot(all_heads(1, rows), features(1 - xl), NN)).astype(BF16)
         outs.append(local(gh_buf.at[rows], gh_hbm.at[rows], LOCAL["gh"] + step))
         if step == 1:
             arrived(cx_got, "c_xh", 0)

time: 58.4 us -> 57.2 us (0.979)
  Pallas kernels: 57 us -> 55.8 us
    pallas_call x1, Pallas kernels: 54.8 us -> 53.6 us  [body(): pl.pallas_call(kernel, out_shape=(jax.ShapeDtypeStruct((TOK, HEADS * HEAD...]
where the time goes in v5:
time: 57.2 us; the launch traced here: 56.4 us
  Pallas kernels  55.8 us (98%)
  between operations  0.64 us (1%)
    pallas_call x1, Pallas kernels, body(): pl.pallas_call(kernel, out_shape=(jax.ShapeDtypeStruct((TOK, HEADS * HEAD...  53.6 us
    pallas_call x1, Pallas kernels, body(): pl.pallas_call(hand_over, out_shape=tuple((jax.ShapeDtypeStruct(r.shape,...  2.16 us

profile of v5, /device:TPU:32, one launch (start us, length us, event | category | flops | bytes accessed | tf_op | source)
XLA Modules:
  0.0 56.4 jit_solution(9339080481844984603)
XLA Ops:
  0.6 53.6 %attention_backward.1 = (bf16[512,512]{1,0:T(8,128)(2,1)}, bf16[512,512]{1,0:T(8,128)(2,1)}, f32[64,512]{1,0:T(8,128)}, f32[64,512]{1,0:T(8,128)}) custom-call(s32[1,8]{1,0:T(1,128)} %len_hbm.1, bf16[512,8192]{1,0:T(8,128)(2,1)} %hid_hbm.1, bf16[512,512]{1,0:T(8,128)(2,1)} %q_hbm.1, bf16[64,512]{1,0:T(8,128)(2,1)} %bitcast.6, bf16[64,512]{1,0:T(8,128)(2,1)} %bitcast.7, ...), custom_call_target="tpu_custom_call" | custom-call | tf_op jit(solution)/shard_map/attention_backward/pallas_call | solution.py:436
  54.3 2.2 %hand_over.1 = (bf16[512,512]{1,0:T(8,128)(2,1)}, bf16[512,512]{1,0:T(8,128)(2,1)}, f32[64,512]{1,0:T(8,128)}, f32[64,512]{1,0:T(8,128)}) custom-call(bf16[512,512]{1,0:T(8,128)(2,1)} %get-tuple-element.12.refs_0_, bf16[512,512]{1,0:T(8,128)(2,1)} %get-tuple-element.13.refs_1_, f32[64,512]{1,0:T(8,128)} %get-tuple-element.14.refs_2_, ...), custom_call_target="tpu_custom_call" | custom-call | tf_op jit(solution)/shard_map/hand_over/pallas_call | solution.py:466
